TPU v7x, 256 devices: a whole 4x4x8 slice. The times are simulated.
256 devices in a mesh: gx: 16 (over z, core), gy: 16 (over y, x).
Axes of the slice: x: 4, y: 4, z: 8, core: 2. Of those that a mesh axis runs over, the one named last changes fastest.
Arguments:
- right_side: float32 [128, 128, 8, 512], P('gx', 'gy'), may hold values from -9 to 9
- kappa_sq: float32 [128, 128, 512], P('gx', 'gy'), may hold values from 0.01 to 2
- coarse_inverse: float32 [4096, 256], P('gx'), may hold values from -0.25 to 32, as said below
Outputs:
- iterate: float32 [128, 128, 8, 512], P('gx', 'gy')
- residual: float32 [128, 128, 8, 512], P('gx', 'gy')
Inputs may be any that keep to these rules, and one draw needn't show every extreme that they name: `coarse_inverse`: each slab's block of 256 rows is a symmetric 256 x 256 matrix; its off-diagonal entries lie within -0.25 to 0.25 and its diagonal entries within 8 to 32.
All inputs are finite; a program needn't handle non-finite values.
Results may differ from a plain program's by a relative error of at most 0.0003.
Values sent between devices are 32-bit elements; how exact they have to be, the bound alone decides.
No kernel may reach another device: no remote copies, remote signals or barrier semaphores. Data moves between devices by JAX's collectives and lax.ppermute only.
A program may use at most 64 MiB of HBM per device.

v0:
```python
import jax
import jax.numpy as jnp
from jax import lax
from jax.sharding import PartitionSpec as P

NCD = 16
ITERS = 2
relax_weight = 2.0 / 3.0


def with_halo(block, sides, width):
    for axis, dim in sides:
        count = lax.axis_size(axis)
        forward = [(i, i + 1) for i in range(count - 1)]
        backward = [(target, source) for source, target in forward]
        low = lax.ppermute(
            lax.slice_in_dim(block, block.shape[dim] - width, None, axis=dim), axis, forward
        )
        high = lax.ppermute(lax.slice_in_dim(block, 0, width, axis=dim), axis, backward)
        block = jnp.concatenate([low, block, high], axis=dim)
    return block


def stencil(padded, field, diag_shift):
    padded = jnp.pad(padded, ((0, 0), (0, 0), (0, 0), (1, 1)))
    beside = padded[2:, 1:-1, :, 1:-1] + padded[:-2, 1:-1, :, 1:-1]
    beside = beside + padded[1:-1, 2:, :, 1:-1] + padded[1:-1, :-2, :, 1:-1]
    beside = beside + padded[1:-1, 1:-1, :, 2:] + padded[1:-1, 1:-1, :, :-2]
    return diag_shift * field - beside


def apply_operator(field, diag_shift):
    padded = with_halo(field, (("gx", 0), ("gy", 1)), 1)
    return stencil(padded, field, diag_shift)


def jacobi_sweep(correction, source, diag_shift):
    return (
        correction + relax_weight * (source - apply_operator(correction, diag_shift)) / diag_shift
    )


def coarse_solve(defect, coarse_inverse):
    width_x, width_y, probes, depth = defect.shape
    zblock = depth // NCD
    blocks = defect.reshape(width_x, width_y, probes, NCD, zblock)
    local_means = jnp.mean(blocks, axis=(0, 1, 4))
    row_start = lax.axis_index("gy") * NCD
    own_rows = lax.dynamic_slice_in_dim(coarse_inverse, row_start, NCD, 0)
    return lax.dot_general(
        lax.all_gather(local_means, "gy", axis=1, tiled=True),
        own_rows,
        (((1,), (1,)), ((), ())),
        precision=lax.Precision.HIGHEST,
        preferred_element_type=jnp.float32,
    )


def prolong(coarse_values, shape):
    width_x, width_y, probes, depth = shape
    zblock = depth // NCD
    spread = jnp.broadcast_to(
        coarse_values[None, None, :, :, None], (width_x, width_y, probes, NCD, zblock)
    )
    return spread.reshape(shape)


def precondition(source, diag_shift, coarse_inverse):
    correction = relax_weight * source / diag_shift
    correction = jacobi_sweep(correction, source, diag_shift)
    defect = source - apply_operator(correction, diag_shift)
    coarse_values = coarse_solve(defect, coarse_inverse)
    coarse_field = prolong(coarse_values, source.shape)
    correction = correction + coarse_field
    correction = jacobi_sweep(correction, source, diag_shift)
    return jacobi_sweep(correction, source, diag_shift)


def probe_dot(first, second):
    return jnp.sum(first * second, axis=(0, 1, 3))


def per_probe(values):
    return values[None, None, :, None]


def energy_sum(residual, precond):
    return lax.psum(probe_dot(residual, precond), ("gx", "gy"))


def body(right_side, kappa_sq, coarse_inverse):
    diag_shift = (6.0 + kappa_sq)[:, :, None, :]
    iterate = jnp.zeros_like(right_side)
    residual = right_side
    precond = precondition(residual, diag_shift, coarse_inverse)
    search = precond
    energy = energy_sum(residual, precond)
    for iteration in range(ITERS):
        op_image = apply_operator(search, diag_shift)
        curvature = lax.psum(probe_dot(search, op_image), ("gx", "gy"))
        step_size = energy / curvature
        iterate = iterate + per_probe(step_size) * search
        residual = residual - per_probe(step_size) * op_image
        if iteration + 1 < ITERS:
            precond = precondition(residual, diag_shift, coarse_inverse)
            energy_next = energy_sum(residual, precond)
            search = precond + per_probe(energy_next / energy) * search
            energy = energy_next
    return (iterate, residual)


def solution(mesh):
    placed = (P("gx", "gy", None, None), P("gx", "gy", None), P("gx", None))
    return jax.shard_map(
        body,
        mesh=mesh,
        in_specs=placed,
        out_specs=(P("gx", "gy", None, None), P("gx", "gy", None, None)),
        check_vma=False,
    )
```

profile of v0, /device:TPU:1, one launch (start us, length us, event | category | flops | bytes accessed | tf_op | source)
XLA Modules:
  0.0 519.5 jit_solution(6656495104835346042)
XLA Ops:
  3.1 4.9 collective-permute-start.1
  10.0 4.3 collective-permute-done
  25.0 4.1 collective-permute-start.5
  31.0 4.3 collective-permute-done.4
  46.0 21.1 %all-gather = f32[16,16,8]{1,2,0:T(8,128)S(1)} all-gather(f32[1,16,8]{1,2,0:T(8,128)S(1)} %multiply_bitcast_fusion.1), channel_id=1, replica_groups=mesh['gx'=16,'gy'=16] {'gy'}, dimensions={0}, use_global_device_ids=true | all-gather | bytes 8704 | tf_op jit(solution)/shard_map/all_gather | solution.py:51
  67.7 9.0 %collective-permute-start.9 = (f32[1,8,8,512]{3,2,1,0:T(8,128)S(1)}, f32[1,8,8,512]{3,2,1,0:T(8,128)S(1)}, u32[]{:S(2)}, u32[]{:S(2)}) collective-permute-start(f32[1,8,8,512]{3,2,1,0:T(8,128)S(1)} %get-tuple-element.47), channel_id=1, source_target_pairs={{0,16},{16,32},{32,48},{48,64},{64,80},{80,96},{96,112},{112,128},... | collective-permute-start | bytes 393224 | tf_op jit(solution)/shard_map/ppermute | solution.py:16
  78.6 4.3 collective-permute-done.8
  92.2 4.7 collective-permute-start.13
  98.8 4.3 collective-permute-done.12
  113.4 4.0 collective-permute-start.17
  119.3 4.3 collective-permute-done.16
  123.7 4.9 collective-permute-start.19
  137.0 84.1 %all-reduce.10 = (f32[8]{0:T(128)S(1)}, f32[8]{0:T(128)S(1)}) all-reduce(f32[8]{0:T(128)S(1)} %get-tuple-element.3, f32[8]{0:T(128)S(1)} %get-tuple-element.2), channel_id=1, replica_groups=mesh['gx'=16,'gy'=16] {'gx','gy'}, use_global_device_ids=true, to_apply=%region_3.4 | all-reduce | flops 16 | bytes 128 | tf_op jit(solution)/shard_map/psum | solution.py:88
  241.3 4.9 collective-permute-start.25
  248.2 4.3 collective-permute-done.24
  257.0 4.3 collective-permute-done.26
  264.1 21.4 %all-gather.1 = f32[16,16,8]{1,2,0:T(8,128)S(1)} all-gather(f32[1,16,8]{1,2,0:T(8,128)S(1)} %multiply_bitcast_fusion), channel_id=1, replica_groups=mesh['gx'=16,'gy'=16] {'gy'}, dimensions={0}, use_global_device_ids=true | all-gather | bytes 8704 | tf_op jit(solution)/shard_map/all_gather | solution.py:51
  289.0 9.9 %collective-permute-start.29 = (f32[1,8,8,512]{3,2,1,0:T(8,128)S(1)}, f32[1,8,8,512]{3,2,1,0:T(8,128)S(1)}, u32[]{:S(2)}, u32[]{:S(2)}) collective-permute-start(f32[1,8,8,512]{3,2,1,0:T(8,128)S(1)} %get-tuple-element.37), channel_id=1, source_target_pairs={{0,16},{16,32},{32,48},{48,64},{64,80},{80,96},{96,112},{112,128},... | collective-permute-start | bytes 393224 | tf_op jit(solution)/shard_map/ppermute | solution.py:16
  300.9 4.3 collective-permute-done.28
  314.0 4.5 collective-permute-start.33
  320.4 4.3 collective-permute-done.32
  337.0 79.8 %psum.30 = f32[8]{0:T(128)S(1)} all-reduce(f32[8]{0:T(128)S(1)} %get-tuple-element.8), channel_id=1, replica_groups=mesh['gx'=16,'gy'=16] {'gx','gy'}, use_global_device_ids=true, to_apply=%region_9.10 | all-reduce | flops 8 | bytes 64 | tf_op jit(solution)/shard_map/psum | solution.py:88
  422.7 3.9 collective-permute-done.36
  436.6 79.8 %psum.31 = f32[8]{0:T(128)S(1)} all-reduce(f32[8]{0:T(128)S(1)} %get-tuple-element.6), channel_id=1, replica_groups=mesh['gx'=16,'gy'=16] {'gx','gy'}, use_global_device_ids=true, to_apply=%region_11.12 | all-reduce | flops 8 | bytes 64 | tf_op jit(solution)/shard_map/psum | solution.py:100
  (139 shorter events, 138.1 us)
Async XLA Ops:
  3.1 6.9 %collective-permute-start.1 = (f32[1,8,8,512]{3,2,1,0:T(8,128)S(1)}, f32[1,8,8,512]{3,2,1,0:T(8,128)S(1)}, u32[]{:S(2)}, u32[]{:S(2)}) collective-permute-start(f32[1,8,8,512]{3,2,1,0:T(8,128)S(1)} %get-tuple-element.51), channel_id=1, source_target_pairs={{0,16},{16,32},{32,48},{48,64},{64,80},{80,96},{96,112},{112,128},... | collective-permute-start | bytes 393224 | tf_op jit(solution)/shard_map/ppermute | solution.py:16
  8.0 6.3 %collective-permute-start = (f32[1,8,8,512]{3,2,1,0:T(8,128)S(1)}, f32[1,8,8,512]{3,2,1,0:T(8,128)S(1)}, u32[]{:S(2)}, u32[]{:S(2)}) collective-permute-start(f32[1,8,8,512]{3,2,1,0:T(8,128)S(1)} %get-tuple-element.52), channel_id=1, source_target_pairs={{16,0},{32,16},{48,32},{64,48},{80,64},{96,80},{112,96},{128,112},... | collective-permute-start | bytes 393224 | tf_op jit(solution)/shard_map/ppermute | solution.py:19
  17.6 6.1 %collective-permute-start.2 = (f32[10,1,8,512]{3,2,1,0:T(8,128)S(1)}, f32[10,1,8,512]{3,2,1,0:T(8,128)S(1)}, u32[]{:S(2)}, u32[]{:S(2)}) collective-permute-start(f32[10,1,8,512]{3,2,1,0:T(8,128)S(1)} %get-tuple-element.32), channel_id=1, source_target_pairs={{1,0},{2,1},{3,2},{4,3},{5,4},{6,5},{7,6},{8,7},{9,8},{10,9},{11,1... | collective-permute-start | bytes 491528 | tf_op jit(solution)/shard_map/ppermute | solution.py:19
  29.1 6.3 %collective-permute-start.4 = (f32[1,8,8,512]{3,2,1,0:T(8,128)S(1)}, f32[1,8,8,512]{3,2,1,0:T(8,128)S(1)}, u32[]{:S(2)}, u32[]{:S(2)}) collective-permute-start(f32[1,8,8,512]{3,2,1,0:T(8,128)S(1)} %get-tuple-element.50), channel_id=1, source_target_pairs={{16,0},{32,16},{48,32},{64,48},{80,64},{96,80},{112,96},{128,112},... | collective-permute-start | bytes 393224 | tf_op jit(solution)/shard_map/ppermute | solution.py:19
  38.5 6.1 %collective-permute-start.6 = (f32[10,1,8,512]{3,2,1,0:T(8,128)S(1)}, f32[10,1,8,512]{3,2,1,0:T(8,128)S(1)}, u32[]{:S(2)}, u32[]{:S(2)}) collective-permute-start(f32[10,1,8,512]{3,2,1,0:T(8,128)S(1)} %get-tuple-element.30), channel_id=1, source_target_pairs={{1,0},{2,1},{3,2},{4,3},{5,4},{6,5},{7,6},{8,7},{9,8},{10,9},{11,1... | collective-permute-start | bytes 491528 | tf_op jit(solution)/shard_map/ppermute | solution.py:19
  67.7 10.9 %collective-permute-start.9 = (f32[1,8,8,512]{3,2,1,0:T(8,128)S(1)}, f32[1,8,8,512]{3,2,1,0:T(8,128)S(1)}, u32[]{:S(2)}, u32[]{:S(2)}) collective-permute-start(f32[1,8,8,512]{3,2,1,0:T(8,128)S(1)} %get-tuple-element.47), channel_id=1, source_target_pairs={{0,16},{16,32},{32,48},{48,64},{64,80},{80,96},{96,112},{112,128},... | collective-permute-start | bytes 393224 | tf_op jit(solution)/shard_map/ppermute | solution.py:16
  76.6 6.3 %collective-permute-start.8 = (f32[1,8,8,512]{3,2,1,0:T(8,128)S(1)}, f32[1,8,8,512]{3,2,1,0:T(8,128)S(1)}, u32[]{:S(2)}, u32[]{:S(2)}) collective-permute-start(f32[1,8,8,512]{3,2,1,0:T(8,128)S(1)} %get-tuple-element.48), channel_id=1, source_target_pairs={{16,0},{32,16},{48,32},{64,48},{80,64},{96,80},{112,96},{128,112},... | collective-permute-start | bytes 393224 | tf_op jit(solution)/shard_map/ppermute | solution.py:19
  84.8 6.1 %collective-permute-start.10 = (f32[10,1,8,512]{3,2,1,0:T(8,128)S(1)}, f32[10,1,8,512]{3,2,1,0:T(8,128)S(1)}, u32[]{:S(2)}, u32[]{:S(2)}) collective-permute-start(f32[10,1,8,512]{3,2,1,0:T(8,128)S(1)} %get-tuple-element.28), channel_id=1, source_target_pairs={{1,0},{2,1},{3,2},{4,3},{5,4},{6,5},{7,6},{8,7},{9,8},{10,9},{11,1... | collective-permute-start | bytes 491528 | tf_op jit(solution)/shard_map/ppermute | solution.py:19
  92.2 6.6 %collective-permute-start.13 = (f32[1,8,8,512]{3,2,1,0:T(8,128)S(1)}, f32[1,8,8,512]{3,2,1,0:T(8,128)S(1)}, u32[]{:S(2)}, u32[]{:S(2)}) collective-permute-start(f32[1,8,8,512]{3,2,1,0:T(8,128)S(1)} %get-tuple-element.45), channel_id=1, source_target_pairs={{0,16},{16,32},{32,48},{48,64},{64,80},{80,96},{96,112},{112,128},... | collective-permute-start | bytes 393224 | tf_op jit(solution)/shard_map/ppermute | solution.py:16
  96.8 6.3 %collective-permute-start.12 = (f32[1,8,8,512]{3,2,1,0:T(8,128)S(1)}, f32[1,8,8,512]{3,2,1,0:T(8,128)S(1)}, u32[]{:S(2)}, u32[]{:S(2)}) collective-permute-start(f32[1,8,8,512]{3,2,1,0:T(8,128)S(1)} %get-tuple-element.46), channel_id=1, source_target_pairs={{16,0},{32,16},{48,32},{64,48},{80,64},{96,80},{112,96},{128,112},... | collective-permute-start | bytes 393224 | tf_op jit(solution)/shard_map/ppermute | solution.py:19
  106.0 6.1 %collective-permute-start.14 = (f32[10,1,8,512]{3,2,1,0:T(8,128)S(1)}, f32[10,1,8,512]{3,2,1,0:T(8,128)S(1)}, u32[]{:S(2)}, u32[]{:S(2)}) collective-permute-start(f32[10,1,8,512]{3,2,1,0:T(8,128)S(1)} %get-tuple-element.26), channel_id=1, source_target_pairs={{1,0},{2,1},{3,2},{4,3},{5,4},{6,5},{7,6},{8,7},{9,8},{10,9},{11,1... | collective-permute-start | bytes 491528 | tf_op jit(solution)/shard_map/ppermute | solution.py:19
  117.4 6.3 %collective-permute-start.16 = (f32[1,8,8,512]{3,2,1,0:T(8,128)S(1)}, f32[1,8,8,512]{3,2,1,0:T(8,128)S(1)}, u32[]{:S(2)}, u32[]{:S(2)}) collective-permute-start(f32[1,8,8,512]{3,2,1,0:T(8,128)S(1)} %get-tuple-element.44), channel_id=1, source_target_pairs={{16,0},{32,16},{48,32},{64,48},{80,64},{96,80},{112,96},{128,112},... | collective-permute-start | bytes 393224 | tf_op jit(solution)/shard_map/ppermute | solution.py:19
  123.7 7.1 %collective-permute-start.19 = (f32[10,1,8,512]{3,2,1,0:T(8,128)S(1)}, f32[10,1,8,512]{3,2,1,0:T(8,128)S(1)}, u32[]{:S(2)}, u32[]{:S(2)}) collective-permute-start(f32[10,1,8,512]{3,2,1,0:T(8,128)S(1)} %get-tuple-element.23), channel_id=1, source_target_pairs={{0,1},{1,2},{2,3},{3,4},{4,5},{5,6},{6,7},{7,8},{8,9},{9,10},{10,1... | collective-permute-start | bytes 491528 | tf_op jit(solution)/shard_map/ppermute | solution.py:16
  128.6 6.1 %collective-permute-start.18 = (f32[10,1,8,512]{3,2,1,0:T(8,128)S(1)}, f32[10,1,8,512]{3,2,1,0:T(8,128)S(1)}, u32[]{:S(2)}, u32[]{:S(2)}) collective-permute-start(f32[10,1,8,512]{3,2,1,0:T(8,128)S(1)} %get-tuple-element.24), channel_id=1, source_target_pairs={{1,0},{2,1},{3,2},{4,3},{5,4},{6,5},{7,6},{8,7},{9,8},{10,9},{11,1... | collective-permute-start | bytes 491528 | tf_op jit(solution)/shard_map/ppermute | solution.py:19
  225.2 6.3 %collective-permute-start.20 = (f32[1,8,8,512]{3,2,1,0:T(8,128)S(1)}, f32[1,8,8,512]{3,2,1,0:T(8,128)S(1)}, u32[]{:S(2)}, u32[]{:S(2)}) collective-permute-start(f32[1,8,8,512]{3,2,1,0:T(8,128)S(1)} %get-tuple-element.42), channel_id=1, source_target_pairs={{16,0},{32,16},{48,32},{64,48},{80,64},{96,80},{112,96},{128,112},... | collective-permute-start | bytes 393224 | tf_op jit(solution)/shard_map/ppermute | solution.py:19
  241.3 6.8 %collective-permute-start.25 = (f32[1,8,8,512]{3,2,1,0:T(8,128)S(1)}, f32[1,8,8,512]{3,2,1,0:T(8,128)S(1)}, u32[]{:S(2)}, u32[]{:S(2)}) collective-permute-start(f32[1,8,8,512]{3,2,1,0:T(8,128)S(1)} %get-tuple-element.39), channel_id=1, source_target_pairs={{0,16},{16,32},{32,48},{48,64},{64,80},{80,96},{96,112},{112,128},... | collective-permute-start | bytes 393224 | tf_op jit(solution)/shard_map/ppermute | solution.py:16
  246.2 6.3 %collective-permute-start.24 = (f32[1,8,8,512]{3,2,1,0:T(8,128)S(1)}, f32[1,8,8,512]{3,2,1,0:T(8,128)S(1)}, u32[]{:S(2)}, u32[]{:S(2)}) collective-permute-start(f32[1,8,8,512]{3,2,1,0:T(8,128)S(1)} %get-tuple-element.40), channel_id=1, source_target_pairs={{16,0},{32,16},{48,32},{64,48},{80,64},{96,80},{112,96},{128,112},... | collective-permute-start | bytes 393224 | tf_op jit(solution)/shard_map/ppermute | solution.py:19
  254.7 6.5 %collective-permute-start.26 = (f32[10,1,8,512]{3,2,1,0:T(8,128)S(1)}, f32[10,1,8,512]{3,2,1,0:T(8,128)S(1)}, u32[]{:S(2)}, u32[]{:S(2)}) collective-permute-start(f32[10,1,8,512]{3,2,1,0:T(8,128)S(1)} %get-tuple-element.20), channel_id=1, source_target_pairs={{1,0},{2,1},{3,2},{4,3},{5,4},{6,5},{7,6},{8,7},{9,8},{10,9},{11,1... | collective-permute-start | bytes 491528 | tf_op jit(solution)/shard_map/ppermute | solution.py:19
  289.0 11.8 %collective-permute-start.29 = (f32[1,8,8,512]{3,2,1,0:T(8,128)S(1)}, f32[1,8,8,512]{3,2,1,0:T(8,128)S(1)}, u32[]{:S(2)}, u32[]{:S(2)}) collective-permute-start(f32[1,8,8,512]{3,2,1,0:T(8,128)S(1)} %get-tuple-element.37), channel_id=1, source_target_pairs={{0,16},{16,32},{32,48},{48,64},{64,80},{80,96},{96,112},{112,128},... | collective-permute-start | bytes 393224 | tf_op jit(solution)/shard_map/ppermute | solution.py:16
  298.9 6.3 %collective-permute-start.28 = (f32[1,8,8,512]{3,2,1,0:T(8,128)S(1)}, f32[1,8,8,512]{3,2,1,0:T(8,128)S(1)}, u32[]{:S(2)}, u32[]{:S(2)}) collective-permute-start(f32[1,8,8,512]{3,2,1,0:T(8,128)S(1)} %get-tuple-element.38), channel_id=1, source_target_pairs={{16,0},{32,16},{48,32},{64,48},{80,64},{96,80},{112,96},{128,112},... | collective-permute-start | bytes 393224 | tf_op jit(solution)/shard_map/ppermute | solution.py:19
  306.6 6.1 %collective-permute-start.30 = (f32[10,1,8,512]{3,2,1,0:T(8,128)S(1)}, f32[10,1,8,512]{3,2,1,0:T(8,128)S(1)}, u32[]{:S(2)}, u32[]{:S(2)}) collective-permute-start(f32[10,1,8,512]{3,2,1,0:T(8,128)S(1)} %get-tuple-element.18), channel_id=1, source_target_pairs={{1,0},{2,1},{3,2},{4,3},{5,4},{6,5},{7,6},{8,7},{9,8},{10,9},{11,1... | collective-permute-start | bytes 491528 | tf_op jit(solution)/shard_map/ppermute | solution.py:19
  314.0 6.4 %collective-permute-start.33 = (f32[1,8,8,512]{3,2,1,0:T(8,128)S(1)}, f32[1,8,8,512]{3,2,1,0:T(8,128)S(1)}, u32[]{:S(2)}, u32[]{:S(2)}) collective-permute-start(f32[1,8,8,512]{3,2,1,0:T(8,128)S(1)} %get-tuple-element.35), channel_id=1, source_target_pairs={{0,16},{16,32},{32,48},{48,64},{64,80},{80,96},{96,112},{112,128},... | collective-permute-start | bytes 393224 | tf_op jit(solution)/shard_map/ppermute | solution.py:16
  318.5 6.3 %collective-permute-start.32 = (f32[1,8,8,512]{3,2,1,0:T(8,128)S(1)}, f32[1,8,8,512]{3,2,1,0:T(8,128)S(1)}, u32[]{:S(2)}, u32[]{:S(2)}) collective-permute-start(f32[1,8,8,512]{3,2,1,0:T(8,128)S(1)} %get-tuple-element.36), channel_id=1, source_target_pairs={{16,0},{32,16},{48,32},{64,48},{80,64},{96,80},{112,96},{128,112},... | collective-permute-start | bytes 393224 | tf_op jit(solution)/shard_map/ppermute | solution.py:19
  420.3 6.3 %collective-permute-start.36 = (f32[1,8,8,512]{3,2,1,0:T(8,128)S(1)}, f32[1,8,8,512]{3,2,1,0:T(8,128)S(1)}, u32[]{:S(2)}, u32[]{:S(2)}) collective-permute-start(f32[1,8,8,512]{3,2,1,0:T(8,128)S(1)} %get-tuple-element.34), channel_id=1, source_target_pairs={{16,0},{32,16},{48,32},{64,48},{80,64},{96,80},{112,96},{128,112},... | collective-permute-start | bytes 393224 | tf_op jit(solution)/shard_map/ppermute | solution.py:19
  (22 other events, 322.9 us)
where the time goes:
time: 521 us; the launch traced here: 519 us
  blocking collectives  286 us (55%)
  starting transfers between devices  110 us (21%)
  waiting for transfers between devices  90.7 us (17%)
  other arithmetic  25.9 us (5%)
    psum x2, blocking collectives, energy_sum(): return lax.psum(probe_dot(residual, precond), ('gx', 'gy'))  164 us
    ppermute x20, waiting for transfers between devices, with_halo(): lax.ppermute(lax.slice_in_dim(block, 0, width, axis=dim), axis, backward)  81.3 us
    psum x1, blocking collectives, body(): curvature = lax.psum(probe_dot(search, op_image), ('gx', 'gy'))  79.8 us
    ppermute x20, starting transfers between devices, with_halo(): lax.ppermute(lax.slice_in_dim(block, block.shape[dim] - width, None, axis...  77 us
    all_gather x2, blocking collectives, coarse_solve(): lax.all_gather(local_means, 'gy', axis=1, tiled=True)  42.5 us
    ppermute x20, starting transfers between devices, with_halo(): lax.ppermute(lax.slice_in_dim(block, 0, width, axis=dim), axis, backward)  33 us
  transfers between devices with their start and end apart: 40, of which 30 were waited for; matrix products, arithmetic and copies ran while one was open for 0% of the time, Pallas kernels for 0%

commit v1 on v0

--- a/solution.py
+++ b/solution.py
@@ -85,7 +85,13 @@
 
 
 def energy_sum(residual, precond):
-    return lax.psum(probe_dot(residual, precond), ("gx", "gy"))
+
+    def _answer_body(original):
+        for ii in ("gy", "gx"):
+            original = lax.psum(original, ii)
+        return original
+
+    return _answer_body(probe_dot(residual, precond))
 
 
 def body(right_side, kappa_sq, coarse_inverse):

time: 521 us -> 561 us (1.077)
  blocking collectives: 286 us -> 325 us
    psum x1 -> x2, blocking collectives: 79.8 us -> 169 us  [body(): curvature = lax.psum(probe_dot(search, op_image), ('gx', 'gy'))]
    psum x2 -> x4, blocking collectives: 164 us -> 114 us  [_answer_body(): original = lax.psum(original, ii)]
where the time goes in v1:
time: 561 us; the launch traced here: 559 us
  blocking collectives  325 us (58%)
  starting transfers between devices  110 us (20%)
  waiting for transfers between devices  90.7 us (16%)
  other arithmetic  25.9 us (5%)
    psum x2, blocking collectives, body(): curvature = lax.psum(probe_dot(search, op_image), ('gx', 'gy'))  169 us
    psum x4, blocking collectives, _answer_body(): original = lax.psum(original, ii)  114 us
    ppermute x20, waiting for transfers between devices, with_halo(): lax.ppermute(lax.slice_in_dim(block, 0, width, axis=dim), axis, backward)  81.1 us
    ppermute x20, starting transfers between devices, with_halo(): lax.ppermute(lax.slice_in_dim(block, block.shape[dim] - width, None, axis...  76.8 us
    all_gather x2, blocking collectives, coarse_solve(): lax.all_gather(local_means, 'gy', axis=1, tiled=True)  42.4 us
    ppermute x20, starting transfers between devices, with_halo(): lax.ppermute(lax.slice_in_dim(block, 0, width, axis=dim), axis, backward)  33.5 us
  transfers between devices with their start and end apart: 40, of which 30 were waited for; matrix products, arithmetic and copies ran while one was open for 0% of the time, Pallas kernels for 0%

profile of v1, /device:TPU:1, one launch (start us, length us, event | category | flops | bytes accessed | tf_op | source)
XLA Modules:
  0.0 558.9 jit_solution(9475435423449159611)
XLA Ops:
  3.1 4.9 collective-permute-start.1
  9.9 4.3 collective-permute-done
  31.0 4.3 collective-permute-done.4
  46.0 21.1 %all-gather = f32[16,16,8]{1,2,0:T(8,128)S(1)} all-gather(f32[1,16,8]{1,2,0:T(8,128)S(1)} %multiply_bitcast_fusion.1), channel_id=1, replica_groups=mesh['gx'=16,'gy'=16] {'gy'}, dimensions={0}, use_global_device_ids=true | all-gather | bytes 8704 | tf_op jit(solution)/shard_map/all_gather | solution.py:51
  67.6 9.0 %collective-permute-start.9 = (f32[1,8,8,512]{3,2,1,0:T(8,128)S(1)}, f32[1,8,8,512]{3,2,1,0:T(8,128)S(1)}, u32[]{:S(2)}, u32[]{:S(2)}) collective-permute-start(f32[1,8,8,512]{3,2,1,0:T(8,128)S(1)} %get-tuple-element.45), channel_id=1, source_target_pairs={{0,16},{16,32},{32,48},{48,64},{64,80},{80,96},{96,112},{112,128},... | collective-permute-start | bytes 393224 | tf_op jit(solution)/shard_map/ppermute | solution.py:16
  78.5 4.3 collective-permute-done.8
  92.1 4.7 collective-permute-start.13
  98.7 4.3 collective-permute-done.12
  119.3 4.3 collective-permute-done.16
  123.7 4.9 collective-permute-start.19
  137.0 30.6 %psum.42 = f32[8]{0:T(128)S(1)} all-reduce(f32[8]{0:T(128)S(1)} %get-tuple-element.3), channel_id=1, replica_groups=mesh['gx'=16,'gy'=16] {'gy'}, use_global_device_ids=true, to_apply=%region_3.4 | all-reduce | flops 8 | bytes 64 | tf_op jit(solution)/shard_map/psum | solution.py:91
  167.6 83.5 %psum.44 = f32[8]{0:T(128)S(1)} all-reduce(f32[8]{0:T(128)S(1)} %get-tuple-element.2), channel_id=1, replica_groups=mesh['gx'=16,'gy'=16] {'gx','gy'}, use_global_device_ids=true, to_apply=%region_6.7 | all-reduce | flops 8 | bytes 64 | tf_op jit(solution)/shard_map/psum | solution.py:106
  251.1 24.0 %psum.43 = f32[8]{0:T(128)S(1)} all-reduce(f32[8]{0:T(128)S(1)} %psum.42), channel_id=1, replica_groups=mesh['gx'=16,'gy'=16] {'gx'}, use_global_device_ids=true, to_apply=%region_4.5 | all-reduce | flops 8 | bytes 64 | tf_op jit(solution)/shard_map/psum | solution.py:91
  292.3 4.1 collective-permute-done.22
  302.2 4.3 collective-permute-done.24
  318.1 21.4 %all-gather.1 = f32[16,16,8]{1,2,0:T(8,128)S(1)} all-gather(f32[1,16,8]{1,2,0:T(8,128)S(1)} %multiply_bitcast_fusion), channel_id=1, replica_groups=mesh['gx'=16,'gy'=16] {'gy'}, dimensions={0}, use_global_device_ids=true | all-gather | bytes 8704 | tf_op jit(solution)/shard_map/all_gather | solution.py:51
  342.9 8.6 %collective-permute-start.29 = (f32[1,8,8,512]{3,2,1,0:T(8,128)S(1)}, f32[1,8,8,512]{3,2,1,0:T(8,128)S(1)}, u32[]{:S(2)}, u32[]{:S(2)}) collective-permute-start(f32[1,8,8,512]{3,2,1,0:T(8,128)S(1)} %get-tuple-element.35), channel_id=1, source_target_pairs={{0,16},{16,32},{32,48},{48,64},{64,80},{80,96},{96,112},{112,128},... | collective-permute-start | bytes 393224 | tf_op jit(solution)/shard_map/ppermute | solution.py:16
  353.4 4.3 collective-permute-done.28
  372.4 4.3 collective-permute-done.32
  388.6 30.1 %psum.45 = f32[8]{0:T(128)S(1)} all-reduce(f32[8]{0:T(128)S(1)} %get-tuple-element.6), channel_id=1, replica_groups=mesh['gx'=16,'gy'=16] {'gy'}, use_global_device_ids=true, to_apply=%region_10.11 | all-reduce | flops 8 | bytes 64 | tf_op jit(solution)/shard_map/psum | solution.py:91
  418.7 29.3 %psum.46 = f32[8]{0:T(128)S(1)} all-reduce(f32[8]{0:T(128)S(1)} %psum.45), channel_id=1, replica_groups=mesh['gx'=16,'gy'=16] {'gx'}, use_global_device_ids=true, to_apply=%region_11.12 | all-reduce | flops 8 | bytes 64 | tf_op jit(solution)/shard_map/psum | solution.py:91
  449.6 4.1 collective-permute-start.37
  455.7 4.3 collective-permute-done.36
  470.5 85.4 %psum.47 = f32[8]{0:T(128)S(1)} all-reduce(f32[8]{0:T(128)S(1)} %get-tuple-element.4), channel_id=1, replica_groups=mesh['gx'=16,'gy'=16] {'gx','gy'}, use_global_device_ids=true, to_apply=%region_13.14 | all-reduce | flops 8 | bytes 64 | tf_op jit(solution)/shard_map/psum | solution.py:106
  (142 shorter events, 152.8 us)
Async XLA Ops:
  3.1 6.9 %collective-permute-start.1 = (f32[1,8,8,512]{3,2,1,0:T(8,128)S(1)}, f32[1,8,8,512]{3,2,1,0:T(8,128)S(1)}, u32[]{:S(2)}, u32[]{:S(2)}) collective-permute-start(f32[1,8,8,512]{3,2,1,0:T(8,128)S(1)} %get-tuple-element.49), channel_id=1, source_target_pairs={{0,16},{16,32},{32,48},{48,64},{64,80},{80,96},{96,112},{112,128},... | collective-permute-start | bytes 393224 | tf_op jit(solution)/shard_map/ppermute | solution.py:16
  8.0 6.3 %collective-permute-start = (f32[1,8,8,512]{3,2,1,0:T(8,128)S(1)}, f32[1,8,8,512]{3,2,1,0:T(8,128)S(1)}, u32[]{:S(2)}, u32[]{:S(2)}) collective-permute-start(f32[1,8,8,512]{3,2,1,0:T(8,128)S(1)} %get-tuple-element.50), channel_id=1, source_target_pairs={{16,0},{32,16},{48,32},{64,48},{80,64},{96,80},{112,96},{128,112},... | collective-permute-start | bytes 393224 | tf_op jit(solution)/shard_map/ppermute | solution.py:19
  29.1 6.3 %collective-permute-start.4 = (f32[1,8,8,512]{3,2,1,0:T(8,128)S(1)}, f32[1,8,8,512]{3,2,1,0:T(8,128)S(1)}, u32[]{:S(2)}, u32[]{:S(2)}) collective-permute-start(f32[1,8,8,512]{3,2,1,0:T(8,128)S(1)} %get-tuple-element.48), channel_id=1, source_target_pairs={{16,0},{32,16},{48,32},{64,48},{80,64},{96,80},{112,96},{128,112},... | collective-permute-start | bytes 393224 | tf_op jit(solution)/shard_map/ppermute | solution.py:19
  38.5 6.1 %collective-permute-start.6 = (f32[10,1,8,512]{3,2,1,0:T(8,128)S(1)}, f32[10,1,8,512]{3,2,1,0:T(8,128)S(1)}, u32[]{:S(2)}, u32[]{:S(2)}) collective-permute-start(f32[10,1,8,512]{3,2,1,0:T(8,128)S(1)} %get-tuple-element.28), channel_id=1, source_target_pairs={{1,0},{2,1},{3,2},{4,3},{5,4},{6,5},{7,6},{8,7},{9,8},{10,9},{11,1... | collective-permute-start | bytes 491528 | tf_op jit(solution)/shard_map/ppermute | solution.py:19
  67.6 10.9 %collective-permute-start.9 = (f32[1,8,8,512]{3,2,1,0:T(8,128)S(1)}, f32[1,8,8,512]{3,2,1,0:T(8,128)S(1)}, u32[]{:S(2)}, u32[]{:S(2)}) collective-permute-start(f32[1,8,8,512]{3,2,1,0:T(8,128)S(1)} %get-tuple-element.45), channel_id=1, source_target_pairs={{0,16},{16,32},{32,48},{48,64},{64,80},{80,96},{96,112},{112,128},... | collective-permute-start | bytes 393224 | tf_op jit(solution)/shard_map/ppermute | solution.py:16
  76.6 6.3 %collective-permute-start.8 = (f32[1,8,8,512]{3,2,1,0:T(8,128)S(1)}, f32[1,8,8,512]{3,2,1,0:T(8,128)S(1)}, u32[]{:S(2)}, u32[]{:S(2)}) collective-permute-start(f32[1,8,8,512]{3,2,1,0:T(8,128)S(1)} %get-tuple-element.46), channel_id=1, source_target_pairs={{16,0},{32,16},{48,32},{64,48},{80,64},{96,80},{112,96},{128,112},... | collective-permute-start | bytes 393224 | tf_op jit(solution)/shard_map/ppermute | solution.py:19
  84.7 6.1 %collective-permute-start.10 = (f32[10,1,8,512]{3,2,1,0:T(8,128)S(1)}, f32[10,1,8,512]{3,2,1,0:T(8,128)S(1)}, u32[]{:S(2)}, u32[]{:S(2)}) collective-permute-start(f32[10,1,8,512]{3,2,1,0:T(8,128)S(1)} %get-tuple-element.26), channel_id=1, source_target_pairs={{1,0},{2,1},{3,2},{4,3},{5,4},{6,5},{7,6},{8,7},{9,8},{10,9},{11,1... | collective-permute-start | bytes 491528 | tf_op jit(solution)/shard_map/ppermute | solution.py:19
  92.1 6.6 %collective-permute-start.13 = (f32[1,8,8,512]{3,2,1,0:T(8,128)S(1)}, f32[1,8,8,512]{3,2,1,0:T(8,128)S(1)}, u32[]{:S(2)}, u32[]{:S(2)}) collective-permute-start(f32[1,8,8,512]{3,2,1,0:T(8,128)S(1)} %get-tuple-element.43), channel_id=1, source_target_pairs={{0,16},{16,32},{32,48},{48,64},{64,80},{80,96},{96,112},{112,128},... | collective-permute-start | bytes 393224 | tf_op jit(solution)/shard_map/ppermute | solution.py:16
  96.8 6.3 %collective-permute-start.12 = (f32[1,8,8,512]{3,2,1,0:T(8,128)S(1)}, f32[1,8,8,512]{3,2,1,0:T(8,128)S(1)}, u32[]{:S(2)}, u32[]{:S(2)}) collective-permute-start(f32[1,8,8,512]{3,2,1,0:T(8,128)S(1)} %get-tuple-element.44), channel_id=1, source_target_pairs={{16,0},{32,16},{48,32},{64,48},{80,64},{96,80},{112,96},{128,112},... | collective-permute-start | bytes 393224 | tf_op jit(solution)/shard_map/ppermute | solution.py:19
  106.0 6.1 %collective-permute-start.14 = (f32[10,1,8,512]{3,2,1,0:T(8,128)S(1)}, f32[10,1,8,512]{3,2,1,0:T(8,128)S(1)}, u32[]{:S(2)}, u32[]{:S(2)}) collective-permute-start(f32[10,1,8,512]{3,2,1,0:T(8,128)S(1)} %get-tuple-element.24), channel_id=1, source_target_pairs={{1,0},{2,1},{3,2},{4,3},{5,4},{6,5},{7,6},{8,7},{9,8},{10,9},{11,1... | collective-permute-start | bytes 491528 | tf_op jit(solution)/shard_map/ppermute | solution.py:19
  117.3 6.3 %collective-permute-start.16 = (f32[1,8,8,512]{3,2,1,0:T(8,128)S(1)}, f32[1,8,8,512]{3,2,1,0:T(8,128)S(1)}, u32[]{:S(2)}, u32[]{:S(2)}) collective-permute-start(f32[1,8,8,512]{3,2,1,0:T(8,128)S(1)} %get-tuple-element.42), channel_id=1, source_target_pairs={{16,0},{32,16},{48,32},{64,48},{80,64},{96,80},{112,96},{128,112},... | collective-permute-start | bytes 393224 | tf_op jit(solution)/shard_map/ppermute | solution.py:19
  123.7 7.1 %collective-permute-start.19 = (f32[10,1,8,512]{3,2,1,0:T(8,128)S(1)}, f32[10,1,8,512]{3,2,1,0:T(8,128)S(1)}, u32[]{:S(2)}, u32[]{:S(2)}) collective-permute-start(f32[10,1,8,512]{3,2,1,0:T(8,128)S(1)} %get-tuple-element.21), channel_id=1, source_target_pairs={{0,1},{1,2},{2,3},{3,4},{4,5},{5,6},{6,7},{7,8},{8,9},{9,10},{10,1... | collective-permute-start | bytes 491528 | tf_op jit(solution)/shard_map/ppermute | solution.py:16
  128.5 6.1 %collective-permute-start.18 = (f32[10,1,8,512]{3,2,1,0:T(8,128)S(1)}, f32[10,1,8,512]{3,2,1,0:T(8,128)S(1)}, u32[]{:S(2)}, u32[]{:S(2)}) collective-permute-start(f32[10,1,8,512]{3,2,1,0:T(8,128)S(1)} %get-tuple-element.22), channel_id=1, source_target_pairs={{1,0},{2,1},{3,2},{4,3},{5,4},{6,5},{7,6},{8,7},{9,8},{10,9},{11,1... | collective-permute-start | bytes 491528 | tf_op jit(solution)/shard_map/ppermute | solution.py:19
  277.2 6.1 %collective-permute-start.21 = (f32[1,8,8,512]{3,2,1,0:T(8,128)S(1)}, f32[1,8,8,512]{3,2,1,0:T(8,128)S(1)}, u32[]{:S(2)}, u32[]{:S(2)}) collective-permute-start(f32[1,8,8,512]{3,2,1,0:T(8,128)S(1)} %get-tuple-element.39), channel_id=1, source_target_pairs={{0,16},{16,32},{32,48},{48,64},{64,80},{80,96},{96,112},{112,128},... | collective-permute-start | bytes 393224 | tf_op jit(solution)/shard_map/ppermute | solution.py:16
  280.2 6.3 %collective-permute-start.20 = (f32[1,8,8,512]{3,2,1,0:T(8,128)S(1)}, f32[1,8,8,512]{3,2,1,0:T(8,128)S(1)}, u32[]{:S(2)}, u32[]{:S(2)}) collective-permute-start(f32[1,8,8,512]{3,2,1,0:T(8,128)S(1)} %get-tuple-element.40), channel_id=1, source_target_pairs={{16,0},{32,16},{48,32},{64,48},{80,64},{96,80},{112,96},{128,112},... | collective-permute-start | bytes 393224 | tf_op jit(solution)/shard_map/ppermute | solution.py:19
  289.7 6.7 %collective-permute-start.22 = (f32[10,1,8,512]{3,2,1,0:T(8,128)S(1)}, f32[10,1,8,512]{3,2,1,0:T(8,128)S(1)}, u32[]{:S(2)}, u32[]{:S(2)}) collective-permute-start(f32[10,1,8,512]{3,2,1,0:T(8,128)S(1)} %get-tuple-element.20), channel_id=1, source_target_pairs={{1,0},{2,1},{3,2},{4,3},{5,4},{6,5},{7,6},{8,7},{9,8},{10,9},{11,1... | collective-permute-start | bytes 491528 | tf_op jit(solution)/shard_map/ppermute | solution.py:19
  300.3 6.3 %collective-permute-start.24 = (f32[1,8,8,512]{3,2,1,0:T(8,128)S(1)}, f32[1,8,8,512]{3,2,1,0:T(8,128)S(1)}, u32[]{:S(2)}, u32[]{:S(2)}) collective-permute-start(f32[1,8,8,512]{3,2,1,0:T(8,128)S(1)} %get-tuple-element.38), channel_id=1, source_target_pairs={{16,0},{32,16},{48,32},{64,48},{80,64},{96,80},{112,96},{128,112},... | collective-permute-start | bytes 393224 | tf_op jit(solution)/shard_map/ppermute | solution.py:19
  308.8 6.3 %collective-permute-start.26 = (f32[10,1,8,512]{3,2,1,0:T(8,128)S(1)}, f32[10,1,8,512]{3,2,1,0:T(8,128)S(1)}, u32[]{:S(2)}, u32[]{:S(2)}) collective-permute-start(f32[10,1,8,512]{3,2,1,0:T(8,128)S(1)} %get-tuple-element.18), channel_id=1, source_target_pairs={{1,0},{2,1},{3,2},{4,3},{5,4},{6,5},{7,6},{8,7},{9,8},{10,9},{11,1... | collective-permute-start | bytes 491528 | tf_op jit(solution)/shard_map/ppermute | solution.py:19
  342.9 10.5 %collective-permute-start.29 = (f32[1,8,8,512]{3,2,1,0:T(8,128)S(1)}, f32[1,8,8,512]{3,2,1,0:T(8,128)S(1)}, u32[]{:S(2)}, u32[]{:S(2)}) collective-permute-start(f32[1,8,8,512]{3,2,1,0:T(8,128)S(1)} %get-tuple-element.35), channel_id=1, source_target_pairs={{0,16},{16,32},{32,48},{48,64},{64,80},{80,96},{96,112},{112,128},... | collective-permute-start | bytes 393224 | tf_op jit(solution)/shard_map/ppermute | solution.py:16
  351.5 6.3 %collective-permute-start.28 = (f32[1,8,8,512]{3,2,1,0:T(8,128)S(1)}, f32[1,8,8,512]{3,2,1,0:T(8,128)S(1)}, u32[]{:S(2)}, u32[]{:S(2)}) collective-permute-start(f32[1,8,8,512]{3,2,1,0:T(8,128)S(1)} %get-tuple-element.36), channel_id=1, source_target_pairs={{16,0},{32,16},{48,32},{64,48},{80,64},{96,80},{112,96},{128,112},... | collective-permute-start | bytes 393224 | tf_op jit(solution)/shard_map/ppermute | solution.py:19
  359.1 6.1 %collective-permute-start.30 = (f32[10,1,8,512]{3,2,1,0:T(8,128)S(1)}, f32[10,1,8,512]{3,2,1,0:T(8,128)S(1)}, u32[]{:S(2)}, u32[]{:S(2)}) collective-permute-start(f32[10,1,8,512]{3,2,1,0:T(8,128)S(1)} %get-tuple-element.16), channel_id=1, source_target_pairs={{1,0},{2,1},{3,2},{4,3},{5,4},{6,5},{7,6},{8,7},{9,8},{10,9},{11,1... | collective-permute-start | bytes 491528 | tf_op jit(solution)/shard_map/ppermute | solution.py:19
  370.4 6.3 %collective-permute-start.32 = (f32[1,8,8,512]{3,2,1,0:T(8,128)S(1)}, f32[1,8,8,512]{3,2,1,0:T(8,128)S(1)}, u32[]{:S(2)}, u32[]{:S(2)}) collective-permute-start(f32[1,8,8,512]{3,2,1,0:T(8,128)S(1)} %get-tuple-element.34), channel_id=1, source_target_pairs={{16,0},{32,16},{48,32},{64,48},{80,64},{96,80},{112,96},{128,112},... | collective-permute-start | bytes 393224 | tf_op jit(solution)/shard_map/ppermute | solution.py:19
  380.1 6.1 %collective-permute-start.34 = (f32[10,1,8,512]{3,2,1,0:T(8,128)S(1)}, f32[10,1,8,512]{3,2,1,0:T(8,128)S(1)}, u32[]{:S(2)}, u32[]{:S(2)}) collective-permute-start(f32[10,1,8,512]{3,2,1,0:T(8,128)S(1)} %get-tuple-element.14), channel_id=1, source_target_pairs={{1,0},{2,1},{3,2},{4,3},{5,4},{6,5},{7,6},{8,7},{9,8},{10,9},{11,1... | collective-permute-start | bytes 491528 | tf_op jit(solution)/shard_map/ppermute | solution.py:19
  453.7 6.3 %collective-permute-start.36 = (f32[1,8,8,512]{3,2,1,0:T(8,128)S(1)}, f32[1,8,8,512]{3,2,1,0:T(8,128)S(1)}, u32[]{:S(2)}, u32[]{:S(2)}) collective-permute-start(f32[1,8,8,512]{3,2,1,0:T(8,128)S(1)} %get-tuple-element.32), channel_id=1, source_target_pairs={{16,0},{32,16},{48,32},{64,48},{80,64},{96,80},{112,96},{128,112},... | collective-permute-start | bytes 393224 | tf_op jit(solution)/shard_map/ppermute | solution.py:19
  (22 other events, 311.1 us)
